TPU v7x, 512 devices: a whole 4x8x8 slice. The times are simulated.
512 devices in a mesh: dp: 32 (over z, x), tensor: 16 (over y, core).
Axes of the slice: x: 4, y: 8, z: 8, core: 2. Of those that a mesh axis runs over, the one named last changes fastest.
Arguments:
- grads_out: bfloat16 [1024, 28672], P('dp'), may hold values from -6 to 6
- inputs: bfloat16 [1024, 8192], P('dp'), may hold values from -6 to 6
- basis_out: bfloat16 [28672, 14336], P('dp', 'tensor'), may hold values from -0.03125 to 0.03125
- basis_in: bfloat16 [8192, 4096], P('tensor', 'dp'), may hold values from -0.0625 to 0.0625
- lengths: int32 [32], P('dp'), may hold values from 1 to 32, as said below
Outputs:
- corrections: float32 [14336, 4096], P('tensor', 'dp')
Inputs may be any that keep to these rules, and one draw needn't show every extreme that they name: `lengths`: every sequence has at least one live token, and some sequence has all 32 slots live.
All inputs are finite; a program needn't handle non-finite values.
Results may differ from a plain program's by a relative error of at most 0.0026.
Values may be sent and summed in bfloat16 or wider, within the bound.
No kernel may reach another device: no remote copies, remote signals or barrier semaphores. Data moves between devices by JAX's collectives and lax.ppermute only.
A program may use at most 64 MiB of HBM per device.

v0:
```python
import jax
import jax.numpy as jnp
from jax import lax
from jax.sharding import PartitionSpec as P


def per_device(grads_out, inputs, basis_out, basis_in, lengths):
    seq_len = grads_out.shape[0]
    positions = jnp.arange(seq_len)
    live = positions[:, None] < lengths[0]
    masked = jnp.where(live, grads_out, jnp.zeros_like(grads_out))
    gathered = lax.all_to_all(masked, "dp", split_axis=1, concat_axis=0, tiled=True)
    partial_sum = jnp.dot(gathered, basis_out, preferred_element_type=jnp.float32)
    rotated = lax.psum(partial_sum, "dp").astype(jnp.bfloat16)
    width_in = inputs.shape[1] // lax.axis_size("tensor")
    column_slab = lax.dynamic_slice_in_dim(inputs, lax.axis_index("tensor") * width_in, width_in, 1)
    partial_in = jnp.dot(
        lax.all_gather(column_slab, "dp", axis=0, tiled=True),
        basis_in,
        preferred_element_type=jnp.float32,
    )
    panel = lax.psum(partial_in, "tensor").astype(jnp.bfloat16)
    row_total = rotated.shape[0]
    sequences = row_total // seq_len
    group_size = 4
    number_of_blocks = sequences // group_size
    rotated_blocks = rotated.reshape(number_of_blocks, group_size, seq_len, rotated.shape[1])
    panel_block_list = panel.reshape(number_of_blocks, group_size, seq_len, panel.shape[1])

    def accumulate(total, pair):
        left_factor, right_factor = pair
        sample_case = jnp.einsum(
            "qjt,qjr->qtr", left_factor, right_factor, preferred_element_type=jnp.float32
        )
        return (total + jnp.sum(sample_case * sample_case, axis=0), None)

    initial_total = jnp.zeros((rotated.shape[1], panel.shape[1]), jnp.float32)
    total, unused = lax.scan(accumulate, initial_total, (rotated_blocks, panel_block_list))
    return total / row_total


def solution(mesh):
    placed = (P("dp", None), P("dp", None), P("dp", "tensor"), P("tensor", "dp"), P("dp"))
    return jax.shard_map(
        per_device, mesh=mesh, in_specs=placed, out_specs=P("tensor", "dp"), check_vma=False
    )
```

profile of v0, /device:TPU:24, one launch (start us, length us, event | category | flops | bytes accessed | tf_op | source)
XLA Modules:
  0.0 366.4 jit_solution(3044291850052730541)
XLA Ops:
  6.5 0.0 copy-start
  7.3 1.7 broadcast_select_fusion
  9.0 1.4 copy.10
  10.4 0.0 copy-start.1
  10.4 13.4 %all-to-all-start = ((bf16[32,32,896]{2,0,1:T(8,128)(2,1)}), bf16[32,32,896]{2,0,1:T(8,128)(2,1)}, u32[]{:S(2)}, u32[]{:S(2)}) async-start(bf16[32,32,896]{2,0,1:T(8,128)(2,1)} %bitcast.19), calls=%async_computation | async-start | bytes 3670016 | tf_op jit(solution)/shard_map/all_to_all | solution.py:12
  23.8 0.0 all-gather.2.cloned.1.call-start
  23.9 1.4 constant_dynamic-slice_fusion
  25.3 0.0 all-gather.2.cloned.1.call-update
  25.3 88.1 %all-gather.2.cloned.1.call-done = bf16[1024,512]{1,0:T(8,128)(2,1)} async-done(((bf16[32,512]{1,0:T(8,128)(2,1)}), bf16[1024,512]{1,0:T(8,128)(2,1)}) %all-gather.2.cloned.1.call-update) | async-done | bytes 1048592 | tf_op jit(solution)/shard_map/all_gather | solution.py:18
  113.4 0.0 copy-done.1
  113.4 1.7 fusion.6
  115.1 50.1 %all-reduce.3 = bf16[1024,128]{1,0:T(8,128)(2,1)S(1)} all-reduce(f32[1024,128]{1,0:T(8,128)S(1)} %fusion.6), channel_id=1, replica_groups=mesh['dp'=32,'tensor'=16] {'tensor'}, use_global_device_ids=true, to_apply=%region_1.2 | all-reduce | flops 131072 | bytes 786432 | tf_op jit(solution)/shard_map/psum | solution.py:22
  165.2 0.0 all-to-all-done
  165.2 0.0 copy-done
  165.2 5.5 %fusion.5 = f32[1024,896]{1,0:T(8,128)} fusion(bf16[1024,896]{1,0:T(8,128)(2,1)} %bitcast.2, bf16[896,896]{1,0:T(8,128)(2,1)S(1)} %copy-done), kind=kOutput, calls=%fused_computation.12 | convolution fusion | flops 1644167168 | bytes 7110656 | tf_op jit(solution)/shard_map/dot_general | solution.py:13
  170.8 175.2 %all-reduce.2 = bf16[1024,896]{1,0:T(8,128)(2,1)} all-reduce(f32[1024,896]{1,0:T(8,128)} %fusion.5), channel_id=1, replica_groups=mesh['dp'=32,'tensor'=16] {'dp'}, use_global_device_ids=true, to_apply=%region_0.1 | all-reduce | flops 917504 | bytes 5505024 | tf_op jit(solution)/shard_map/psum | solution.py:14
  346.0 12.8 %while.11 = (s32[]{:T(128)}, f32[896,128]{1,0:T(8,128)S(1)}, bf16[8,4,32,896]{3,2,1,0:T(8,128)(2,1)}, bf16[8,4,32,128]{3,2,1,0:T(8,128)(2,1)S(1)}, s32[]{:T(128)}, /*index=5*/s32[]{:T(128)}) while((s32[]{:T(128)}, f32[896,128]{1,0:T(8,128)S(1)}, bf16[8,4,32,896]{3,2,1,0:T(8,128)(2,1)}, bf16[8,4,32,128]{3,2,1,0:T(8,128)(2,1)S(1)}, ...), condition=%wide.region_4.5_spmd.clone, body=%wide.region_2.4_spmd.clone.sunk | while | flops 30392320 | bytes 2098263 | solution.py:38
  346.0 1.4 multiply_reduce_fusion.2
  347.4 0.1 select_add_fusion.2
  347.6 1.4 multiply_reduce_fusion.2
  349.0 0.1 select_add_fusion.2
  349.2 1.4 multiply_reduce_fusion.2
  350.6 0.1 select_add_fusion.2
  350.8 1.4 multiply_reduce_fusion.2
  352.2 0.1 select_add_fusion.2
  352.4 1.4 multiply_reduce_fusion.2
  353.8 0.1 select_add_fusion.2
  354.0 1.4 multiply_reduce_fusion.2
  355.4 0.1 select_add_fusion.2
  355.6 1.4 multiply_reduce_fusion.2
  357.0 0.1 select_add_fusion.2
  357.2 1.4 multiply_reduce_fusion.2
  358.6 0.1 select_add_fusion.2
  358.7 0.8 broadcast_multiply_fusion
  (2 shorter events, 0.0 us)
Async XLA Ops:
  6.5 158.7 %copy-start = (bf16[896,896]{1,0:T(8,128)(2,1)S(1)}, bf16[896,896]{1,0:T(8,128)(2,1)}, u32[]{:S(2)}) copy-start(bf16[896,896]{1,0:T(8,128)(2,1)} %param.9) | copy-start | bytes 4816900
  10.4 103.0 %copy-start.1 = (bf16[512,128]{1,0:T(8,128)(2,1)S(1)}, bf16[512,128]{1,0:T(8,128)(2,1)}, u32[]{:S(2)}) copy-start(bf16[512,128]{1,0:T(8,128)(2,1)} %param.10) | copy-start | bytes 393220
  10.4 154.8 %all-to-all-start = ((bf16[32,32,896]{2,0,1:T(8,128)(2,1)}), bf16[32,32,896]{2,0,1:T(8,128)(2,1)}, u32[]{:S(2)}, u32[]{:S(2)}) async-start(bf16[32,32,896]{2,0,1:T(8,128)(2,1)} %bitcast.19), calls=%async_computation | async-start | bytes 3670016 | tf_op jit(solution)/shard_map/all_to_all | solution.py:12
  23.8 89.6 %all-gather.2.cloned.1.call-start = ((), (), s32[]{:S(2)}) async-start(), calls=%async_computation.1 | async-start | bytes 1081344 | tf_op jit(solution)/shard_map/all_gather | solution.py:18
Sparse Core Ops, SparseCore 0:
  27.9 85.5 all-gather.1
where the time goes:
time: 367 us; the launch traced here: 366 us
  blocking collectives  225 us (61%)
  waiting for transfers between devices  88.1 us (24%)
  matrix products  18.8 us (5%)
  between operations  14.2 us (4%)
  starting transfers between devices  13.5 us (4%)
    psum x1, blocking collectives, per_device(): rotated = lax.psum(partial_sum, 'dp').astype(jnp.bfloat16)  175 us
    all_gather x1, waiting for transfers between devices, per_device(): lax.all_gather(column_slab, 'dp', axis=0, tiled=True)  88.1 us
    psum x1, blocking collectives, per_device(): panel = lax.psum(partial_in, 'tensor').astype(jnp.bfloat16)  50.1 us
    all_to_all x1, starting transfers between devices, per_device(): lax.all_to_all(masked, 'dp', split_axis=1, concat_axis=0, tiled=True)  13.4 us
    dot_general x8, matrix products, accumulate(): jnp.einsum('qjt,qjr->qtr', left_factor, right_factor, preferred_element_t...  11.6 us
  transfers between devices with their start and end apart: 2, of which 1 were waited for; matrix products, arithmetic and copies ran while one was open for 1% of the time, Pallas kernels for 0%

commit v1 on v0

--- a/solution.py
+++ b/solution.py
@@ -14,11 +14,20 @@
     rotated = lax.psum(partial_sum, "dp").astype(jnp.bfloat16)
     width_in = inputs.shape[1] // lax.axis_size("tensor")
     column_slab = lax.dynamic_slice_in_dim(inputs, lax.axis_index("tensor") * width_in, width_in, 1)
-    partial_in = jnp.dot(
-        lax.all_gather(column_slab, "dp", axis=0, tiled=True),
-        basis_in,
-        preferred_element_type=jnp.float32,
-    )
+
+    def launch_ways(buf):
+        local_next = jnp.concatenate(
+            lax.all_to_all(
+                jnp.stack([buf] * lax.psum(1, axis_name="dp")),
+                axis_name="dp",
+                split_axis=0,
+                concat_axis=0,
+            ),
+            0,
+        )
+        return local_next
+
+    partial_in = jnp.dot(launch_ways(column_slab), basis_in, preferred_element_type=jnp.float32)
     panel = lax.psum(partial_in, "tensor").astype(jnp.bfloat16)
     row_total = rotated.shape[0]
     sequences = row_total // seq_len

time: 367 us -> 300 us (0.82)
  waiting for transfers between devices: 88.1 us -> 24.3 us
  between operations: 14.2 us -> 0.73 us
  starting transfers between devices: 13.5 us -> 19 us
  blocking collectives: 225 us -> 230 us
    all_gather x1 -> x0, waiting for transfers between devices: 88.1 us -> none  [per_device(): lax.all_gather(column_slab, 'dp', axis=0, tiled=True)]
    all_to_all x0 -> x1, waiting for transfers between devices: none -> 24.3 us  [launch_ways(): lax.all_to_all(jnp.stack([buf] * lax.psum(1, axis_name='dp')), axis_name=...]
    all_to_all x0 -> x1, starting transfers between devices: none -> 13.2 us  [launch_ways(): lax.all_to_all(jnp.stack([buf] * lax.psum(1, axis_name='dp')), axis_name=...]
    all_to_all x1, starting transfers between devices: 13.4 us -> 5.79 us  [per_device(): lax.all_to_all(masked, 'dp', split_axis=1, concat_axis=0, tiled=True)]
where the time goes in v1:
time: 300 us
  blocking collectives  230 us (77%)
  waiting for transfers between devices  24.3 us (8%)
  starting transfers between devices  19 us (6%)
  matrix products  18.4 us (6%)
  other arithmetic  3.45 us (1%)
  local copies, waits for them, and re-layouts  3.41 us (1%)
    psum x1, blocking collectives, per_device(): rotated = lax.psum(partial_sum, 'dp').astype(jnp.bfloat16)  177 us
    psum x1, blocking collectives, per_device(): panel = lax.psum(partial_in, 'tensor').astype(jnp.bfloat16)  53 us
    all_to_all x1, waiting for transfers between devices, launch_ways(): lax.all_to_all(jnp.stack([buf] * lax.psum(1, axis_name='dp')), axis_name=...  24.3 us
    all_to_all x1, starting transfers between devices, launch_ways(): lax.all_to_all(jnp.stack([buf] * lax.psum(1, axis_name='dp')), axis_name=...  13.2 us
    dot_general x8, matrix products, accumulate(): jnp.einsum('qjt,qjr->qtr', left_factor, right_factor, preferred_element_t...  11.6 us
  transfers between devices with their start and end apart: 2, of which 1 were waited for; matrix products, arithmetic and copies ran while one was open for 1% of the time, Pallas kernels for 0%

profile of v1, /device:TPU:24, one launch (start us, length us, event | category | flops | bytes accessed | tf_op | source)
XLA Modules:
  0.0 299.6 jit_solution(2615055594585570711)
XLA Ops:
  0.0 0.0 copy-start
  0.0 0.9 constant_dynamic-slice_fusion
  0.9 1.1 stack.2
  2.0 13.2 %all-to-all-start.1 = ((bf16[32,32,512]{2,1,0:T(8,128)(2,1)}), bf16[32,32,512]{2,1,0:T(8,128)(2,1)S(1)}, u32[]{:S(2)}, u32[]{:S(2)}) async-start(bf16[32,32,512]{2,1,0:T(8,128)(2,1)} %stack.2), calls=%async_computation.1 | async-start | bytes 2097152 | tf_op jit(solution)/shard_map/all_to_all | solution.py:20
  15.8 1.7 broadcast_select_fusion
  17.5 1.4 copy.10
  18.9 24.3 %all-to-all-done.1 = bf16[32,32,512]{2,1,0:T(8,128)(2,1)S(1)} async-done(((bf16[32,32,512]{2,1,0:T(8,128)(2,1)}), bf16[32,32,512]{2,1,0:T(8,128)(2,1)S(1)}, u32[]{:S(2)}, u32[]{:S(2)}) %all-to-all-start.1) | async-done | bytes 1048608 | tf_op jit(solution)/shard_map/all_to_all | solution.py:20
  43.3 0.0 copy-start.1
  43.3 5.8 %all-to-all-start = ((bf16[32,32,896]{2,0,1:T(8,128)(2,1)}), bf16[32,32,896]{2,0,1:T(8,128)(2,1)}, u32[]{:S(2)}, u32[]{:S(2)}) async-start(bf16[32,32,896]{2,0,1:T(8,128)(2,1)} %bitcast.20), calls=%async_computation | async-start | bytes 3670016 | tf_op jit(solution)/shard_map/all_to_all | solution.py:12
  49.1 0.0 copy-done.1
  49.1 1.2 fusion.6
  50.3 53.0 %all-reduce.3 = bf16[1024,128]{1,0:T(8,128)(2,1)S(1)} all-reduce(f32[1024,128]{1,0:T(8,128)} %fusion.6), channel_id=1, replica_groups=mesh['dp'=32,'tensor'=16] {'tensor'}, use_global_device_ids=true, to_apply=%region_1.2 | all-reduce | flops 131072 | bytes 786432 | tf_op jit(solution)/shard_map/psum | solution.py:31
  103.4 0.0 all-to-all-done
  103.4 0.0 copy-done
  103.4 5.5 %fusion.5 = f32[1024,896]{1,0:T(8,128)} fusion(bf16[1024,896]{1,0:T(8,128)(2,1)} %bitcast.2, bf16[896,896]{1,0:T(8,128)(2,1)S(1)} %copy-done), kind=kOutput, calls=%fused_computation.12 | convolution fusion | flops 1644167168 | bytes 7110656 | tf_op jit(solution)/shard_map/dot_general | solution.py:13
  108.9 177.0 %all-reduce.2 = bf16[1024,896]{1,0:T(8,128)(2,1)} all-reduce(f32[1024,896]{1,0:T(8,128)} %fusion.5), channel_id=1, replica_groups=mesh['dp'=32,'tensor'=16] {'dp'}, use_global_device_ids=true, to_apply=%region_0.1 | all-reduce | flops 917504 | bytes 5505024 | tf_op jit(solution)/shard_map/psum | solution.py:14
  286.0 12.8 %while.11 = (s32[]{:T(128)}, f32[896,128]{1,0:T(8,128)S(1)}, bf16[8,4,32,896]{3,2,1,0:T(8,128)(2,1)}, bf16[8,4,32,128]{3,2,1,0:T(8,128)(2,1)S(1)}, s32[]{:T(128)}, /*index=5*/s32[]{:T(128)}) while((s32[]{:T(128)}, f32[896,128]{1,0:T(8,128)S(1)}, bf16[8,4,32,896]{3,2,1,0:T(8,128)(2,1)}, bf16[8,4,32,128]{3,2,1,0:T(8,128)(2,1)S(1)}, ...), condition=%wide.region_4.5_spmd.clone, body=%wide.region_2.4_spmd.clone.sunk | while | flops 30392320 | bytes 2098263 | solution.py:47
  286.0 1.4 multiply_reduce_fusion.2
  287.4 0.1 select_add_fusion.2
  287.6 1.4 multiply_reduce_fusion.2
  289.0 0.1 select_add_fusion.2
  289.2 1.4 multiply_reduce_fusion.2
  290.6 0.1 select_add_fusion.2
  290.8 1.4 multiply_reduce_fusion.2
  292.2 0.1 select_add_fusion.2
  292.4 1.4 multiply_reduce_fusion.2
  293.8 0.1 select_add_fusion.2
  294.0 1.4 multiply_reduce_fusion.2
  295.4 0.1 select_add_fusion.2
  295.6 1.4 multiply_reduce_fusion.2
  297.0 0.1 select_add_fusion.2
  297.2 1.4 multiply_reduce_fusion.2
  298.6 0.1 select_add_fusion.2
  298.8 0.8 broadcast_multiply_fusion
  (2 shorter events, 0.0 us)
Async XLA Ops:
  0.0 103.4 %copy-start = (bf16[896,896]{1,0:T(8,128)(2,1)S(1)}, bf16[896,896]{1,0:T(8,128)(2,1)}, u32[]{:S(2)}) copy-start(bf16[896,896]{1,0:T(8,128)(2,1)} %param.9) | copy-start | bytes 4816900
  2.0 41.3 %all-to-all-start.1 = ((bf16[32,32,512]{2,1,0:T(8,128)(2,1)}), bf16[32,32,512]{2,1,0:T(8,128)(2,1)S(1)}, u32[]{:S(2)}, u32[]{:S(2)}) async-start(bf16[32,32,512]{2,1,0:T(8,128)(2,1)} %stack.2), calls=%async_computation.1 | async-start | bytes 2097152 | tf_op jit(solution)/shard_map/all_to_all | solution.py:20
  43.3 5.8 %copy-start.1 = (bf16[512,128]{1,0:T(8,128)(2,1)S(1)}, bf16[512,128]{1,0:T(8,128)(2,1)}, u32[]{:S(2)}) copy-start(bf16[512,128]{1,0:T(8,128)(2,1)} %param.10) | copy-start | bytes 393220
  43.3 60.1 %all-to-all-start = ((bf16[32,32,896]{2,0,1:T(8,128)(2,1)}), bf16[32,32,896]{2,0,1:T(8,128)(2,1)}, u32[]{:S(2)}, u32[]{:S(2)}) async-start(bf16[32,32,896]{2,0,1:T(8,128)(2,1)} %bitcast.20), calls=%async_computation | async-start | bytes 3670016 | tf_op jit(solution)/shard_map/all_to_all | solution.py:12
